TPU v7x, 256 devices: a whole 4x4x8 slice. The times are simulated.
256 devices in a mesh: rows: 4 (over x), chan: 8 (over y, z_lo), filt: 8 (over z_hi, core).
Axes of the slice: x: 4, y: 4, z: 8 (z_hi: 4, z_lo: 2; z = z_hi * 2 + z_lo), core: 2. Of those that a mesh axis runs over, the one named last changes fastest.
Arguments:
- images: bfloat16 [16, 2048, 2048], P('rows', 'chan', 'filt'), may hold values from -6 to 6
- first_weight: bfloat16 [2048, 1024], P('chan', 'filt'), may hold values from -0.125 to 0.125
- group_weight: bfloat16 [3, 3, 32, 1024], P(None, None, None, 'filt'), may hold values from -0.375 to 0.375
- third_weight: bfloat16 [1024, 2048], P('chan', 'filt'), may hold values from -0.1875 to 0.1875
- out_grad: bfloat16 [16, 2048, 2048], P('rows', 'chan', 'filt'), may hold values from -6 to 6
Outputs:
- block_out: bfloat16 [16, 2048, 2048], P('rows', 'chan', 'filt')
- images_grad: float32 [16, 2048, 2048], P('rows', 'chan', 'filt')
- first_grad: float32 [2048, 1024], P('chan', 'filt')
- group_grad: float32 [3, 3, 32, 1024], P(None, None, None, 'filt')
- third_grad: float32 [1024, 2048], P('chan', 'filt')
All inputs are finite; a program needn't handle non-finite values.
Results may differ from a plain program's by a relative error of at most 0.006.
Values may be sent and summed in bfloat16 or wider, within the bound.
No kernel may reach another device: no remote copies, remote signals or barrier semaphores. Data moves between devices by JAX's collectives and lax.ppermute only.
A program may use at most 128 MiB of HBM per device.

v0:
```python
import jax
import jax.numpy as jnp
from jax import lax
from jax.sharding import PartitionSpec as P


def extended(block, sides, width):
    for axis, dim in sides:
        count = lax.axis_size(axis)
        forward = [(i, i + 1) for i in range(count - 1)]
        backward = [(target, source) for source, target in forward]
        low = lax.ppermute(
            lax.slice_in_dim(block, block.shape[dim] - width, None, axis=dim), axis, forward
        )
        high = lax.ppermute(lax.slice_in_dim(block, 0, width, axis=dim), axis, backward)
        block = jnp.concatenate([low, block, high], axis=dim)
    return block


def silu_slope(values):
    logistic = jax.nn.sigmoid(values)
    return logistic * (1.0 + values * (1.0 - logistic))


def group_conv(padded, kernel, groups_here):
    result = lax.conv_general_dilated(
        padded[None],
        kernel,
        (1, 1),
        "VALID",
        dimension_numbers=("NHWC", "HWIO", "NHWC"),
        feature_group_count=groups_here,
        preferred_element_type=jnp.float32,
    )
    return result[0]


def transposed_kernel(kernel, group_size, groups_here):
    pieces = kernel.reshape(3, 3, group_size, groups_here, group_size)
    swapped = jnp.transpose(pieces, (0, 1, 4, 3, 2)).reshape(
        3, 3, group_size, groups_here * group_size
    )
    return swapped[::-1, ::-1]


def kernel_partial(padded_first, group_delta, group_size, groups_here):
    rows_here = group_delta.shape[0]
    cols_here = group_delta.shape[1]
    pixels = rows_here * cols_here
    delta_groups = group_delta.reshape(pixels, groups_here, group_size)
    kernel_terms = []
    for row_shift in range(3):
        for col_shift in range(3):
            window = padded_first[
                row_shift : row_shift + rows_here, col_shift : col_shift + cols_here
            ]
            window = window.reshape(pixels, groups_here, group_size)
            kernel_terms.append(
                jnp.einsum("pgi,pgo->gio", window, delta_groups, preferred_element_type=jnp.float32)
            )
    kernel_part = jnp.stack(kernel_terms).reshape(3, 3, groups_here, group_size, group_size)
    kernel_part = jnp.transpose(kernel_part, (0, 1, 3, 2, 4))
    return kernel_part.reshape(3, 3, group_size, groups_here * group_size)


def body(images, first_weight, group_weight, third_weight, out_grad):
    rows_here = images.shape[0]
    cols_here = images.shape[1]
    group_size = group_weight.shape[2]
    first_panel, third_panel = (
        lax.all_gather(first_weight, "chan", axis=0, tiled=True),
        lax.all_gather(third_weight, "chan", axis=0, tiled=True),
    )
    pixels = rows_here * cols_here
    groups_here = group_weight.shape[3] // group_size
    gathered = lax.all_gather(images, "filt", axis=2, tiled=True)
    flat_images = gathered.reshape(pixels, gathered.shape[2])
    pre_first = jnp.dot(flat_images, first_panel, preferred_element_type=jnp.float32)
    act_first = (
        jax.nn.silu(pre_first)
        .astype(jnp.bfloat16)
        .reshape(rows_here, cols_here, first_panel.shape[1])
    )
    padded_first = extended(act_first, (("rows", 0), ("chan", 1)), 1)
    pre_group = group_conv(padded_first, group_weight, groups_here)
    act_group = jax.nn.silu(pre_group).astype(jnp.bfloat16)
    mid_whole = lax.all_gather(act_group, "filt", axis=2, tiled=True)
    flat_mid = mid_whole.reshape(pixels, mid_whole.shape[2])
    third_out = jnp.dot(flat_mid, third_panel, preferred_element_type=jnp.float32)
    own_images = images.reshape(pixels, images.shape[2]).astype(jnp.float32)
    block_out = (own_images + third_out).astype(jnp.bfloat16).reshape(images.shape)
    grad_flat = out_grad.reshape(pixels, out_grad.shape[2])
    mid_terms = lax.dot_general(
        grad_flat, third_panel, (((1,), (1,)), ((), ())), preferred_element_type=jnp.float32
    )
    mid_grad = lax.psum_scatter(
        mid_terms.reshape(rows_here, cols_here, mid_terms.shape[1]),
        "filt",
        scatter_dimension=2,
        tiled=True,
    )
    third_part = lax.dot_general(
        flat_mid, grad_flat, (((0,), (0,)), ((), ())), preferred_element_type=jnp.float32
    )
    group_delta = (mid_grad * silu_slope(pre_group)).astype(jnp.bfloat16)
    padded_delta = extended(group_delta, (("rows", 0), ("chan", 1)), 1)
    first_back = group_conv(
        padded_delta, transposed_kernel(group_weight, group_size, groups_here), groups_here
    )
    kernel_part = kernel_partial(padded_first, group_delta, group_size, groups_here)
    first_delta = (first_back.reshape(pixels, first_back.shape[2]) * silu_slope(pre_first)).astype(
        jnp.bfloat16
    )
    first_part = lax.dot_general(
        flat_images, first_delta, (((0,), (0,)), ((), ())), preferred_element_type=jnp.float32
    )
    input_terms = lax.dot_general(
        first_delta, first_panel, (((1,), (1,)), ((), ())), preferred_element_type=jnp.float32
    )
    back_images = lax.psum_scatter(
        input_terms.reshape(rows_here, cols_here, input_terms.shape[1]).astype(jnp.bfloat16),
        "filt",
        scatter_dimension=2,
        tiled=True,
    ).astype(jnp.float32)
    images_grad = out_grad.astype(jnp.float32) + back_images
    group_grad = lax.psum(kernel_part, ("rows", "chan"))
    first_total, third_total = lax.psum((first_part, third_part), "rows")
    first_grad, third_grad = (
        lax.psum_scatter(first_total, "chan", scatter_dimension=0, tiled=True),
        lax.psum_scatter(third_total, "chan", scatter_dimension=0, tiled=True),
    )
    return (block_out, images_grad, first_grad, group_grad, third_grad)


def solution(mesh):
    in_specs = (
        P("rows", "chan", "filt"),
        P("chan", "filt"),
        P(None, None, None, "filt"),
        P("chan", "filt"),
        P("rows", "chan", "filt"),
    )
    out_specs = (
        P("rows", "chan", "filt"),
        P("rows", "chan", "filt"),
        P("chan", "filt"),
        P(None, None, None, "filt"),
        P("chan", "filt"),
    )
    return jax.shard_map(body, mesh=mesh, in_specs=in_specs, out_specs=out_specs, check_vma=False)
```

profile of v0, /device:TPU:32, one launch (start us, length us, event | category | flops | bytes accessed | tf_op | source)
XLA Modules:
  0.0 700.0 jit_solution(2654013649618200023)
XLA Ops:
  7.9 39.6 %all_gather.15 = bf16[1024,256]{1,0:T(8,128)(2,1)S(1)} all-gather(bf16[128,256]{1,0:T(8,128)(2,1)} %param.8), channel_id=1, replica_groups=mesh['rows'=4,'chan'=8,'filt'=8] {'chan'}, dimensions={0}, use_global_device_ids=true | all-gather | bytes 589824 | tf_op jit(solution)/shard_map/all_gather | solution.py:72
  47.5 3.8 fusion.10
  52.2 36.9 %all_gather.13 = bf16[2048,128]{1,0:T(8,128)(2,1)S(1)} all-gather(bf16[256,128]{1,0:T(8,128)(2,1)S(1)} %copy-done.13), channel_id=1, replica_groups=mesh['rows'=4,'chan'=8,'filt'=8] {'chan'}, dimensions={0}, use_global_device_ids=true | all-gather | bytes 589824 | tf_op jit(solution)/shard_map/all_gather | solution.py:71
  89.1 4.4 multiply_convert_fusion.3
  93.5 2.9 collective-permute-start
  96.4 1.3 collective-permute-start.1
  98.4 4.2 collective-permute-done.1
  103.2 3.4 collective-permute-start.2
  106.6 3.2 collective-permute-start.3
  110.7 8.0 %collective-permute-done.2 = bf16[6,1,128]{1,2,0:T(8,128)(2,1)S(1)} collective-permute-done((bf16[6,1,128]{1,2,0:T(8,128)(2,1)S(1)}, bf16[6,1,128]{1,2,0:T(8,128)(2,1)S(1)}, u32[]{:S(2)}, u32[]{:S(2)}) %collective-permute-start.2) | collective-permute-done | bytes 1568 | tf_op jit(solution)/shard_map/ppermute | solution.py:12
  118.7 10.6 %collective-permute-done.3 = bf16[6,1,128]{1,2,0:T(8,128)(2,1)S(1)} collective-permute-done((bf16[6,1,128]{1,2,0:T(8,128)(2,1)S(1)}, bf16[6,1,128]{1,2,0:T(8,128)(2,1)S(1)}, u32[]{:S(2)}, u32[]{:S(2)}) %collective-permute-start.3) | collective-permute-done | bytes 1568 | tf_op jit(solution)/shard_map/ppermute | solution.py:15
  130.0 5.8 copy.36
  135.8 9.4 %fusion.13 = f32[1,4,256,4,32]{4,0,3,2,1:T(1,128)S(1)} fusion(bf16[1,6,258,4,32]{4,0,3,2,1:T(2,128)(2,1)} %copy.36, bf16[3,3,32,4,32]{4,3,2,1,0:T(4,128)(2,1)} %shard_map.94), kind=kOutput, calls=%fused_computation.39 | convolution fusion | flops 75497472 | bytes 994304 | tf_op jit(solution)/shard_map/conv_general_dilated | solution.py:26
  145.3 3.5 copy.38
  148.8 1.3 copy.40
  150.2 2.0 multiply_convert_fusion.1
  152.2 3.3 collective-permute-start.4
  155.6 1.3 collective-permute-start.5
  157.5 4.3 collective-permute-done.5
  161.8 3.5 collective-permute-start.6
  165.3 2.6 collective-permute-start.7
  169.2 2.5 collective-permute-done.7
  172.1 5.9 copy.44
  178.0 13.8 %convolution_reduce_fusion = f32[4,256,4,32]{3,2,1,0:T(4,128)S(1)} fusion(bf16[1,6,258,4,32]{4,0,3,2,1:T(2,128)(2,1)} %copy.44, bf16[3,3,32,4,32]{4,3,2,1,0:T(4,128)(2,1)} %rev.6), kind=kOutput, calls=%fused_computation.2 | convolution fusion | flops 75497472 | bytes 994304 | tf_op jit(solution)/shard_map/conv_general_dilated | solution.py:26
  191.8 1.7 reshape.99
  193.5 1.4 multiply_convert_fusion
  194.9 4.0 convolution_bitcast_fusion
  199.0 3.4 convolution_bitcast_fusion.1
  202.4 40.0 %reduce-scatter.9.cloned.1.call-done = f32[256,128]{0,1:T(8,128)} async-done(((f32[2048,128]{0,1:T(8,128)}), f32[256,128]{0,1:T(8,128)}) %reduce-scatter.9.cloned.1.call-update) | async-done | bytes 131088 | tf_op jit(solution)/shard_map/reduce_scatter | solution.py:130
  242.4 44.5 %reduce-scatter.11.cloned.1.call-done = f32[128,256]{1,0:T(8,128)} async-done(((f32[1024,256]{1,0:T(8,128)}), f32[128,256]{1,0:T(8,128)}) %reduce-scatter.11.cloned.1.call-update) | async-done | bytes 131088 | tf_op jit(solution)/shard_map/reduce_scatter | solution.py:131
  286.9 3.2 convolution_convert_fusion
  291.8 1.2 pad_maximum_fusion.1
  294.3 1.8 reshape.85
  297.0 1.1 reshape.88
  299.1 1.8 reshape.89
  302.2 1.1 reshape.91
  304.2 1.1 reshape.93
  306.2 1.1 reshape.86
  307.3 1.1 fusion.9
  308.9 1.2 fusion.6
  311.5 0.9 reshape.95
  312.5 3.2 fusion
  315.6 21.3 %all-reduce.6.cloned.1.call-done = (f32[256,128]{0,1:T(8,128)}, f32[128,256]{1,0:T(8,128)}) async-done(((f32[256,128]{0,1:T(8,128)}, f32[128,256]{1,0:T(8,128)}), (f32[256,128]{0,1:T(8,128)}, f32[128,256]{1,0:T(8,128)})) %all-reduce.6.cloned.1.call-update) | async-done | bytes 262160 | tf_op jit(solution)/shard_map/psum | solution.py:128
  337.0 1.7 copy.60
  338.7 59.3 %reduce-scatter.7.cloned.1.call-done = bf16[4,256,256]{2,1,0:T(8,128)(2,1)} async-done(((bf16[4,256,2048]{2,1,0:T(8,128)(2,1)}), bf16[4,256,256]{2,1,0:T(8,128)(2,1)}) %reduce-scatter.7.cloned.1.call-update) | async-done | bytes 524304 | tf_op jit(solution)/shard_map/reduce_scatter | solution.py:120
  398.0 2.1 convert_add_fusion
  400.1 290.7 %all-reduce.4.cloned.1.call-done = f32[3,3,32,128]{3,2,1,0:T(8,128)} async-done(((f32[3,3,32,128]{3,2,1,0:T(8,128)}), f32[3,3,32,128]{3,2,1,0:T(8,128)}) %all-reduce.4.cloned.1.call-update) | async-done | bytes 147472 | tf_op jit(solution)/shard_map/psum | solution.py:127
  690.9 1.6 copy.78
  (90 shorter events, 17.4 us)
Async XLA Ops:
  7.2 81.9 %all-gather.3.cloned.1.call-start = ((), (), s32[]{:S(2)}) async-start(), calls=%async_computation.4 | async-start | bytes 4718592 | tf_op jit(solution)/shard_map/all_gather | solution.py:76
  7.9 142.2 %reduce-scatter.5.cloned.1.call-start = ((), (), s32[]{:S(2)}) async-start(), calls=%async_computation.6 | async-start | bytes 4718592 | tf_op jit(solution)/shard_map/reduce_scatter | solution.py:96
  51.3 0.8 copy-start.13
  51.4 147.6 %all-gather.5.cloned.1.call-start = ((), (), s32[]{:S(2)}) async-start(), calls=%async_computation.5 | async-start | bytes 2359296 | tf_op jit(solution)/shard_map/all_gather | solution.py:87
  89.1 4.4 copy-start
  93.5 16.3 %copy-start.12 = (bf16[3,3,32,128]{3,2,1,0:T(8,128)(2,1)S(1)}, bf16[3,3,32,128]{3,2,1,0:T(8,128)(2,1)}, u32[]{:S(2)}) copy-start(bf16[3,3,32,128]{3,2,1,0:T(8,128)(2,1)} %param.7) | copy-start | bytes 221188
  93.5 4.8 collective-permute-start
  96.4 6.2 collective-permute-start.1
  98.3 4.6 copy-start.7
  102.6 0.6 copy-start.9
  103.2 15.5 %collective-permute-start.2 = (bf16[6,1,128]{1,2,0:T(8,128)(2,1)S(1)}, bf16[6,1,128]{1,2,0:T(8,128)(2,1)S(1)}, u32[]{:S(2)}, u32[]{:S(2)}) collective-permute-start(bf16[6,1,128]{1,2,0:T(8,128)(2,1)S(1)} %get-tuple-element.29), channel_id=1, source_target_pairs={{0,8},{8,16},{16,24},{24,32},{32,40},{40,48},{48,56},{1,9},{9,17},... | collective-permute-start | bytes 4616 | tf_op jit(solution)/shard_map/ppermute | solution.py:12
  106.6 22.7 %collective-permute-start.3 = (bf16[6,1,128]{1,2,0:T(8,128)(2,1)S(1)}, bf16[6,1,128]{1,2,0:T(8,128)(2,1)S(1)}, u32[]{:S(2)}, u32[]{:S(2)}) collective-permute-start(bf16[6,1,128]{1,2,0:T(8,128)(2,1)S(1)} %get-tuple-element.30), channel_id=1, source_target_pairs={{8,0},{16,8},{24,16},{32,24},{40,32},{48,40},{56,48},{9,1},{17,9},... | collective-permute-start | bytes 4616 | tf_op jit(solution)/shard_map/ppermute | solution.py:15
  118.7 17.1 %copy-start.4 = (bf16[6,1,128]{1,2,0:T(8,128)(2,1)}, bf16[6,1,128]{1,2,0:T(8,128)(2,1)S(1)}, u32[]{:S(2)}) copy-start(bf16[6,1,128]{1,2,0:T(8,128)(2,1)S(1)} %collective-permute-done.2) | copy-start | bytes 4612
  129.3 0.7 copy-start.6
  148.8 19.0 %copy-start.3 = (bf16[3,3,32,4,32]{4,3,2,1,0:T(4,128)(2,1)S(1)}, bf16[3,3,32,4,32]{4,3,2,1,0:T(4,128)(2,1)}, u32[]{:S(2)}) copy-start(bf16[3,3,32,4,32]{4,3,2,1,0:T(4,128)(2,1)} %shard_map.94) | copy-start | bytes 221188
  152.2 90.2 %reduce-scatter.9.cloned.1.call-start = ((), (), s32[]{:S(2)}) async-start(), calls=%async_computation.9 | async-start | bytes 1179648 | tf_op jit(solution)/shard_map/reduce_scatter | solution.py:130
  152.2 5.2 collective-permute-start.4
  155.6 6.2 collective-permute-start.5
  161.8 7.4 %collective-permute-start.6 = (bf16[6,1,128]{2,1,0:T(2,128)(2,1)S(1)}, bf16[6,1,128]{2,1,0:T(2,128)(2,1)S(1)}, u32[]{:S(2)}, u32[]{:S(2)}) collective-permute-start(bf16[6,1,128]{2,1,0:T(2,128)(2,1)S(1)} %get-tuple-element.27), channel_id=1, source_target_pairs={{0,8},{8,16},{16,24},{24,32},{32,40},{40,48},{48,56},{1,9},{9,17},... | collective-permute-start | bytes 4616 | tf_op jit(solution)/shard_map/ppermute | solution.py:12
  165.3 6.4 collective-permute-start.7
  194.9 4.1 copy-start.2
  198.9 88.0 %copy-start.1 = (bf16[2048,128]{1,0:T(8,128)(2,1)S(1)}, bf16[2048,128]{1,0:T(8,128)(2,1)}, u32[]{:S(2)}) copy-start(bf16[2048,128]{1,0:T(8,128)(2,1)} %copy-done) | copy-start | bytes 1572868
  198.9 88.0 %reduce-scatter.11.cloned.1.call-start = ((), (), s32[]{:S(2)}) async-start(), calls=%async_computation.10 | async-start | bytes 1179648 | tf_op jit(solution)/shard_map/reduce_scatter | solution.py:131
  202.4 134.6 %all-reduce.6.cloned.1.call-start = ((), (), s32[]{:S(2)}) async-start(), calls=%async_computation.11 | async-start | bytes 524288 | tf_op jit(solution)/shard_map/psum | solution.py:128
  286.9 111.1 %reduce-scatter.7.cloned.1.call-start = ((), (), s32[]{:S(2)}) async-start(), calls=%async_computation.7 | async-start | bytes 4718592 | tf_op jit(solution)/shard_map/reduce_scatter | solution.py:120
  290.2 0.8 copy-start.8
  290.2 0.9 copy-start.10
  290.2 1.6 copy-start.5
  290.2 400.7 %all-reduce.4.cloned.1.call-start = ((), (), s32[]{:S(2)}) async-start(), calls=%async_computation.8 | async-start | bytes 294912 | tf_op jit(solution)/shard_map/psum | solution.py:127
  337.0 355.5 %copy-start.11 = (f32[128,256]{1,0:T(8,128)S(1)}, f32[128,256]{1,0:T(8,128)}, u32[]{:S(2)}) copy-start(f32[128,256]{1,0:T(8,128)} %get-tuple-element.46) | copy-start | bytes 393220
Sparse Core Ops, SparseCore 0:
  9.8 60.3 all-gather.2
  72.7 76.7 reduce-scatter.4
  152.3 42.8 all-gather.4
  199.0 43.3 reduce-scatter.8
  244.8 42.0 reduce-scatter.10
  289.1 47.8 all-reduce.5
  339.7 58.2 reduce-scatter.6
  401.4 289.4 all-reduce.3
where the time goes:
time: 701 us; the launch traced here: 700 us
  waiting for transfers between devices  487 us (69%)
  blocking collectives  76.5 us (11%)
  matrix products  49 us (7%)
  local copies, waits for them, and re-layouts  43.4 us (6%)
  starting transfers between devices  22 us (3%)
  between operations  14.5 us (2%)
  other arithmetic  7.29 us (1%)
    psum x1, waiting for transfers between devices, body(): group_grad = lax.psum(kernel_part, ('rows', 'chan'))  291 us
    reduce_scatter x1, waiting for transfers between devices, body(): lax.psum_scatter(input_terms.reshape(rows_here, cols_here, input_terms.sh...  59.3 us
    reduce_scatter x1, waiting for transfers between devices, body(): lax.psum_scatter(third_total, 'chan', scatter_dimension=0, tiled=True)  44.5 us
    reduce_scatter x1, waiting for transfers between devices, body(): lax.psum_scatter(first_total, 'chan', scatter_dimension=0, tiled=True)  40 us
    all_gather x1, blocking collectives, body(): lax.all_gather(third_weight, 'chan', axis=0, tiled=True)  39.6 us
    all_gather x1, blocking collectives, body(): lax.all_gather(first_weight, 'chan', axis=0, tiled=True)  36.9 us
    conv_general_dilated x2, matrix products, group_conv(): lax.conv_general_dilated(padded[None], kernel, (1, 1), 'VALID', dimension...  23.3 us
    ppermute x4, waiting for transfers between devices, extended(): lax.ppermute(lax.slice_in_dim(block, 0, width, axis=dim), axis, backward)  21.5 us
  transfers between devices with their start and end apart: 16, of which 12 were waited for; matrix products, arithmetic and copies ran while one was open for 13% of the time, Pallas kernels for 0%

commit v1 on v0

--- a/solution.py
+++ b/solution.py
@@ -2,6 +2,13 @@
 import jax.numpy as jnp
 from jax import lax
 from jax.sharding import PartitionSpec as P
+from jax.lax import psum
+
+
+def find_positions_now(axis_name, named_axis, patch):
+    for dev_j in (axis_name, named_axis):
+        patch = psum(patch, axis_name=dev_j)
+    return patch
 
 
 def extended(block, sides, width):
@@ -124,7 +131,7 @@
         tiled=True,
     ).astype(jnp.float32)
     images_grad = out_grad.astype(jnp.float32) + back_images
-    group_grad = lax.psum(kernel_part, ("rows", "chan"))
+    group_grad = find_positions_now("chan", "rows", kernel_part)
     first_total, third_total = lax.psum((first_part, third_part), "rows")
     first_grad, third_grad = (
         lax.psum_scatter(first_total, "chan", scatter_dimension=0, tiled=True),

time: 701 us -> 486 us (0.69)
  waiting for transfers between devices: 487 us -> 286 us
  local copies, waits for them, and re-layouts: 43.4 us -> 31.1 us
    psum x1, waiting for transfers between devices: 291 us -> 60.2 us  [find_positions_now(): patch = psum(patch, axis_name=dev_j)]
    psum x1, waiting for transfers between devices: 21.3 us -> 43.7 us  [body(): first_total, third_total = lax.psum((first_part, third_part), 'rows')]
  transfers between devices with their start and end apart: 16 -> 16, of which waited for: 12 -> 12; matrix products, arithmetic and copies ran while one was open for 13% -> 16% of each run, Pallas kernels for 0% -> 0%
where the time goes in v1:
time: 486 us; the launch traced here: 482 us
  waiting for transfers between devices  286 us (59%)
  blocking collectives  75.7 us (16%)
  matrix products  47 us (10%)
  local copies, waits for them, and re-layouts  31.1 us (6%)
  starting transfers between devices  22.6 us (5%)
  between operations  14.7 us (3%)
  other arithmetic  5.17 us (1%)
    psum x1, waiting for transfers between devices, find_positions_now(): patch = psum(patch, axis_name=dev_j)  60.2 us
    reduce_scatter x1, waiting for transfers between devices, body(): lax.psum_scatter(input_terms.reshape(rows_here, cols_here, input_terms.sh...  59.3 us
    reduce_scatter x1, waiting for transfers between devices, body(): lax.psum_scatter(first_total, 'chan', scatter_dimension=0, tiled=True)  45.2 us
    reduce_scatter x1, waiting for transfers between devices, body(): lax.psum_scatter(third_total, 'chan', scatter_dimension=0, tiled=True)  44.5 us
    psum x1, waiting for transfers between devices, body(): first_total, third_total = lax.psum((first_part, third_part), 'rows')  43.7 us
    all_gather x1, blocking collectives, body(): lax.all_gather(third_weight, 'chan', axis=0, tiled=True)  39.6 us
    all_gather x1, blocking collectives, body(): lax.all_gather(first_weight, 'chan', axis=0, tiled=True)  36.2 us
    conv_general_dilated x2, matrix products, group_conv(): lax.conv_general_dilated(padded[None], kernel, (1, 1), 'VALID', dimension...  23.2 us
  transfers between devices with their start and end apart: 16, of which 12 were waited for; matrix products, arithmetic and copies ran while one was open for 16% of the time, Pallas kernels for 0%

profile of v1, /device:TPU:32, one launch (start us, length us, event | category | flops | bytes accessed | tf_op | source)
XLA Modules:
  0.0 482.3 jit_solution(7897267235663076131)
XLA Ops:
  7.2 0.7 all-gather.3.cloned.1.call-update
  7.9 39.6 %all_gather.15 = bf16[1024,256]{1,0:T(8,128)(2,1)S(1)} all-gather(bf16[128,256]{1,0:T(8,128)(2,1)} %param.8), channel_id=1, replica_groups=mesh['rows'=4,'chan'=8,'filt'=8] {'chan'}, dimensions={0}, use_global_device_ids=true | all-gather | bytes 589824 | tf_op jit(solution)/shard_map/all_gather | solution.py:79
  47.5 0.8 copy-done
  48.3 3.8 fusion.10
  52.2 0.8 copy-done.21
  53.0 36.2 %all_gather.13 = bf16[2048,128]{1,0:T(8,128)(2,1)S(1)} all-gather(bf16[256,128]{1,0:T(8,128)(2,1)S(1)} %copy-done.21), channel_id=1, replica_groups=mesh['rows'=4,'chan'=8,'filt'=8] {'chan'}, dimensions={0}, use_global_device_ids=true | all-gather | bytes 589824 | tf_op jit(solution)/shard_map/all_gather | solution.py:78
  89.1 4.4 multiply_convert_fusion.3
  93.6 2.7 collective-permute-start
  96.2 1.3 collective-permute-start.1
  97.7 0.4 collective-permute-done
  98.2 4.2 collective-permute-done.1
  102.7 3.8 collective-permute-start.2
  106.5 3.1 collective-permute-start.3
  109.8 8.9 %collective-permute-done.2 = bf16[6,1,128]{1,2,0:T(8,128)(2,1)S(1)} collective-permute-done((bf16[6,1,128]{1,2,0:T(8,128)(2,1)S(1)}, bf16[6,1,128]{1,2,0:T(8,128)(2,1)S(1)}, u32[]{:S(2)}, u32[]{:S(2)}) %collective-permute-start.2) | collective-permute-done | bytes 1568 | tf_op jit(solution)/shard_map/ppermute | solution.py:19
  118.7 11.7 %collective-permute-done.3 = bf16[6,1,128]{1,2,0:T(8,128)(2,1)S(1)} collective-permute-done((bf16[6,1,128]{1,2,0:T(8,128)(2,1)S(1)}, bf16[6,1,128]{1,2,0:T(8,128)(2,1)S(1)}, u32[]{:S(2)}, u32[]{:S(2)}) %collective-permute-start.3) | collective-permute-done | bytes 1568 | tf_op jit(solution)/shard_map/ppermute | solution.py:22
  130.5 0.3 pad_maximum_fusion
  130.8 5.9 %copy.36 = bf16[1,6,258,4,32]{4,0,3,2,1:T(2,128)(2,1)} copy(bf16[1,6,258,4,32]{2,4,3,1,0:T(8,128)(2,1)S(1)} %bitcast.121) | data formatting | bytes 792576 | tf_op jit(solution)/shard_map/broadcast_in_dim | solution.py:34
  136.7 9.4 %fusion.13 = f32[1,4,256,4,32]{4,0,3,2,1:T(1,128)S(1)} fusion(bf16[1,6,258,4,32]{4,0,3,2,1:T(2,128)(2,1)} %copy.36, bf16[3,3,32,4,32]{4,3,2,1,0:T(4,128)(2,1)S(1)} %shard_map.94), kind=kOutput, calls=%fused_computation.39 | convolution fusion | flops 75497472 | bytes 994304 | tf_op jit(solution)/shard_map/conv_general_dilated | solution.py:33
  146.1 1.6 copy.38
  147.9 1.2 reduce-scatter.5.cloned.1.call-done
  149.2 2.0 multiply_convert_fusion.1
  151.9 0.9 rev.6
  157.2 3.9 collective-permute-start.4
  161.1 1.3 collective-permute-start.5
  164.0 3.2 collective-permute-done.5
  167.2 3.9 collective-permute-start.6
  171.2 1.9 collective-permute-start.7
  173.3 0.4 copy.58
  173.7 0.9 reshape.95
  175.0 2.6 collective-permute-done.7
  177.7 1.1 copy.42
  178.7 6.9 %copy.44 = bf16[1,6,258,4,32]{4,0,3,2,1:T(2,128)(2,1)S(1)} copy(bf16[1,6,258,4,32]{2,4,3,1,0:T(8,128)(2,1)} %bitcast.120) | data formatting | bytes 792576 | tf_op jit(solution)/shard_map/broadcast_in_dim | solution.py:34
  185.7 13.8 %convolution_reduce_fusion = f32[4,256,4,32]{3,2,1,0:T(4,128)} fusion(bf16[1,6,258,4,32]{4,0,3,2,1:T(2,128)(2,1)S(1)} %copy.44, bf16[3,3,32,4,32]{4,3,2,1,0:T(4,128)(2,1)S(1)} %copy-done.13), kind=kOutput, calls=%fused_computation.2 | convolution fusion | flops 75497472 | bytes 994304 | tf_op jit(solution)/shard_map/conv_general_dilated | solution.py:33
  199.5 2.5 reshape.99
  202.2 4.0 convolution_bitcast_fusion
  206.3 3.4 convolution_bitcast_fusion.1
  209.8 60.2 %all-reduce.4.cloned.1.call-done = f32[3,3,32,128]{3,2,1,0:T(8,128)} async-done(((f32[3,3,32,128]{3,2,1,0:T(8,128)}), f32[3,3,32,128]{3,2,1,0:T(8,128)}) %all-reduce.4.cloned.1.call-update) | async-done | bytes 147472 | tf_op jit(solution)/shard_map/psum | solution.py:10
  270.0 45.2 %reduce-scatter.9.cloned.1.call-done = f32[256,128]{0,1:T(8,128)} async-done(((f32[2048,128]{0,1:T(8,128)}), f32[256,128]{0,1:T(8,128)}) %reduce-scatter.9.cloned.1.call-update) | async-done | bytes 131088 | tf_op jit(solution)/shard_map/reduce_scatter | solution.py:137
  315.2 44.5 %reduce-scatter.11.cloned.1.call-done = f32[128,256]{1,0:T(8,128)} async-done(((f32[1024,256]{1,0:T(8,128)}), f32[128,256]{1,0:T(8,128)}) %reduce-scatter.11.cloned.1.call-update) | async-done | bytes 131088 | tf_op jit(solution)/shard_map/reduce_scatter | solution.py:138
  359.8 3.2 convolution_convert_fusion
  363.1 1.0 copy-done.1
  364.2 3.1 fusion
  367.3 43.7 %all-reduce.6.cloned.1.call-done = (f32[256,128]{0,1:T(8,128)}, f32[3,3,32,128]{3,2,1,0:T(8,128)}, f32[128,256]{1,0:T(8,128)}) async-done(((f32[256,128]{0,1:T(8,128)}, f32[3,3,32,128]{3,2,1,0:T(8,128)}, f32[128,256]{1,0:T(8,128)}), (f32[256,128]{0,1:T(8,128)}, f32[3,3,32,128]{3,2,1,0:T(8,128)}, f32[128,256]{1,0:T(8,128)})) %all-reduce.6.cloned.1.call-update) | async-done | bytes 409616 | tf_op jit(solution)/shard_map/psum | solution.py:135
  411.0 1.7 copy.60
  412.7 59.3 %reduce-scatter.7.cloned.1.call-done = bf16[4,256,256]{2,1,0:T(8,128)(2,1)} async-done(((bf16[4,256,2048]{2,1,0:T(8,128)(2,1)}), bf16[4,256,256]{2,1,0:T(8,128)(2,1)}) %reduce-scatter.7.cloned.1.call-update) | async-done | bytes 524304 | tf_op jit(solution)/shard_map/reduce_scatter | solution.py:127
  472.0 2.1 convert_add_fusion
  474.1 0.7 copy.79
  474.8 0.7 copy.80
  (106 shorter events, 8.9 us)
Async XLA Ops:
  7.2 82.0 %all-gather.3.cloned.1.call-start = ((), (), s32[]{:S(2)}) async-start(), calls=%async_computation.4 | async-start | bytes 4718592 | tf_op jit(solution)/shard_map/all_gather | solution.py:83
  7.9 141.3 %reduce-scatter.5.cloned.1.call-start = ((), (), s32[]{:S(2)}) async-start(), calls=%async_computation.6 | async-start | bytes 4718592 | tf_op jit(solution)/shard_map/reduce_scatter | solution.py:103
  47.5 0.8 copy-start
  52.1 0.8 copy-start.21
  52.2 154.1 %all-gather.5.cloned.1.call-start = ((), (), s32[]{:S(2)}) async-start(), calls=%async_computation.5 | async-start | bytes 2359296 | tf_op jit(solution)/shard_map/all_gather | solution.py:94
  89.1 4.4 copy-start.2
  93.6 16.0 %copy-start.20 = (bf16[3,3,32,128]{3,2,1,0:T(8,128)(2,1)S(1)}, bf16[3,3,32,128]{3,2,1,0:T(8,128)(2,1)}, u32[]{:S(2)}) copy-start(bf16[3,3,32,128]{3,2,1,0:T(8,128)(2,1)} %param.7) | copy-start | bytes 221188
  93.6 4.5 collective-permute-start
  96.2 6.2 %collective-permute-start.1 = (bf16[1,256,128]{2,1,0:T(8,128)(2,1)S(1)}, bf16[1,256,128]{2,1,0:T(8,128)(2,1)S(1)}, u32[]{:S(2)}, u32[]{:S(2)}) collective-permute-start(bf16[1,256,128]{2,1,0:T(8,128)(2,1)S(1)} %get-tuple-element.37), channel_id=1, source_target_pairs={{64,0},{128,64},{192,128},{65,1},{129,65},{193,129},{66,2},{130,66... | collective-permute-start | bytes 196616 | tf_op jit(solution)/shard_map/ppermute | solution.py:22
  98.1 8.4 %copy-start.14 = (bf16[1,256,128]{2,1,0:T(8,128)(2,1)}, bf16[1,256,128]{2,1,0:T(8,128)(2,1)S(1)}, u32[]{:S(2)}) copy-start(bf16[1,256,128]{2,1,0:T(8,128)(2,1)S(1)} %collective-permute-done) | copy-start | bytes 196612
  102.4 4.1 copy-start.16
  102.7 16.0 %collective-permute-start.2 = (bf16[6,1,128]{1,2,0:T(8,128)(2,1)S(1)}, bf16[6,1,128]{1,2,0:T(8,128)(2,1)S(1)}, u32[]{:S(2)}, u32[]{:S(2)}) collective-permute-start(bf16[6,1,128]{1,2,0:T(8,128)(2,1)S(1)} %get-tuple-element.30), channel_id=1, source_target_pairs={{0,8},{8,16},{16,24},{24,32},{32,40},{40,48},{48,56},{1,9},{9,17},... | collective-permute-start | bytes 4616 | tf_op jit(solution)/shard_map/ppermute | solution.py:19
  106.5 23.9 %collective-permute-start.3 = (bf16[6,1,128]{1,2,0:T(8,128)(2,1)S(1)}, bf16[6,1,128]{1,2,0:T(8,128)(2,1)S(1)}, u32[]{:S(2)}, u32[]{:S(2)}) collective-permute-start(bf16[6,1,128]{1,2,0:T(8,128)(2,1)S(1)} %get-tuple-element.31), channel_id=1, source_target_pairs={{8,0},{16,8},{24,16},{32,24},{40,32},{48,40},{56,48},{9,1},{17,9},... | collective-permute-start | bytes 4616 | tf_op jit(solution)/shard_map/ppermute | solution.py:22
  109.8 26.9 %copy-start.5 = (bf16[3,3,32,4,32]{4,3,2,1,0:T(4,128)(2,1)}, bf16[3,3,32,4,32]{4,3,2,1,0:T(4,128)(2,1)S(1)}, u32[]{:S(2)}) copy-start(bf16[3,3,32,4,32]{4,3,2,1,0:T(4,128)(2,1)S(1)} %shard_map.94) | copy-start | bytes 221188
  118.7 18.0 %copy-start.7 = (bf16[6,1,128]{1,2,0:T(8,128)(2,1)}, bf16[6,1,128]{1,2,0:T(8,128)(2,1)S(1)}, u32[]{:S(2)}) copy-start(bf16[6,1,128]{1,2,0:T(8,128)(2,1)S(1)} %collective-permute-done.2) | copy-start | bytes 4612
  130.5 6.2 %copy-start.9 = (bf16[6,1,128]{1,2,0:T(8,128)(2,1)}, bf16[6,1,128]{1,2,0:T(8,128)(2,1)S(1)}, u32[]{:S(2)}) copy-start(bf16[6,1,128]{1,2,0:T(8,128)(2,1)S(1)} %collective-permute-done.3) | copy-start | bytes 4612
  147.7 3.8 copy-start.6
  147.9 5.1 %copy-start.15 = (bf16[1,256,128]{2,1,0:T(8,128)(2,1)S(1)}, bf16[1,256,128]{2,1,0:T(8,128)(2,1)}, u32[]{:S(2)}) copy-start(bf16[1,256,128]{2,1,0:T(8,128)(2,1)} %copy-done.14) | copy-start | bytes 196612
  147.9 5.1 %copy-start.17 = (bf16[1,256,128]{2,1,0:T(8,128)(2,1)S(1)}, bf16[1,256,128]{2,1,0:T(8,128)(2,1)}, u32[]{:S(2)}) copy-start(bf16[1,256,128]{2,1,0:T(8,128)(2,1)} %copy-done.16) | copy-start | bytes 196612
  151.2 118.8 %all-reduce.4.cloned.1.call-start = ((), (), s32[]{:S(2)}) async-start(), calls=%async_computation.8 | async-start | bytes 294912 | tf_op jit(solution)/shard_map/psum | solution.py:10
  151.9 1.9 copy-start.8
  151.9 1.9 copy-start.10
  157.2 6.8 %collective-permute-start.4 = (bf16[1,256,128]{2,1,0:T(8,128)(2,1)S(1)}, bf16[1,256,128]{2,1,0:T(8,128)(2,1)S(1)}, u32[]{:S(2)}, u32[]{:S(2)}) collective-permute-start(bf16[1,256,128]{2,1,0:T(8,128)(2,1)S(1)} %get-tuple-element.34), channel_id=1, source_target_pairs={{0,64},{64,128},{128,192},{1,65},{65,129},{129,193},{2,66},{66,130... | collective-permute-start | bytes 196616 | tf_op jit(solution)/shard_map/ppermute | solution.py:19
  161.1 6.2 %collective-permute-start.5 = (bf16[1,256,128]{2,1,0:T(8,128)(2,1)S(1)}, bf16[1,256,128]{2,1,0:T(8,128)(2,1)S(1)}, u32[]{:S(2)}, u32[]{:S(2)}) collective-permute-start(bf16[1,256,128]{2,1,0:T(8,128)(2,1)S(1)} %get-tuple-element.35), channel_id=1, source_target_pairs={{64,0},{128,64},{192,128},{65,1},{129,65},{193,129},{66,2},{130,66... | collective-permute-start | bytes 196616 | tf_op jit(solution)/shard_map/ppermute | solution.py:22
  167.2 7.8 %collective-permute-start.6 = (bf16[6,1,128]{2,1,0:T(2,128)(2,1)S(1)}, bf16[6,1,128]{2,1,0:T(2,128)(2,1)S(1)}, u32[]{:S(2)}, u32[]{:S(2)}) collective-permute-start(bf16[6,1,128]{2,1,0:T(2,128)(2,1)S(1)} %get-tuple-element.28), channel_id=1, source_target_pairs={{0,8},{8,16},{16,24},{24,32},{32,40},{40,48},{48,56},{1,9},{9,17},... | collective-permute-start | bytes 4616 | tf_op jit(solution)/shard_map/ppermute | solution.py:19
  171.2 6.4 %collective-permute-start.7 = (bf16[6,1,128]{2,1,0:T(2,128)(2,1)S(1)}, bf16[6,1,128]{2,1,0:T(2,128)(2,1)S(1)}, u32[]{:S(2)}, u32[]{:S(2)}) collective-permute-start(bf16[6,1,128]{2,1,0:T(2,128)(2,1)S(1)} %get-tuple-element.29), channel_id=1, source_target_pairs={{8,0},{16,8},{24,16},{32,24},{40,32},{48,40},{56,48},{9,1},{17,9},... | collective-permute-start | bytes 4616 | tf_op jit(solution)/shard_map/ppermute | solution.py:22
  174.7 140.5 %reduce-scatter.9.cloned.1.call-start = ((), (), s32[]{:S(2)}) async-start(), calls=%async_computation.9 | async-start | bytes 1179648 | tf_op jit(solution)/shard_map/reduce_scatter | solution.py:137
  178.7 6.9 %copy-start.13 = (bf16[3,3,32,4,32]{4,3,2,1,0:T(4,128)(2,1)S(1)}, bf16[3,3,32,4,32]{4,3,2,1,0:T(4,128)(2,1)}, u32[]{:S(2)}) copy-start(bf16[3,3,32,4,32]{4,3,2,1,0:T(4,128)(2,1)} %rev.6) | copy-start | bytes 221188
  199.5 2.5 copy-start.12
  202.2 4.1 copy-start.4
  206.2 153.6 %copy-start.3 = (bf16[2048,128]{1,0:T(8,128)(2,1)S(1)}, bf16[2048,128]{1,0:T(8,128)(2,1)}, u32[]{:S(2)}) copy-start(bf16[2048,128]{1,0:T(8,128)(2,1)} %copy-done.2) | copy-start | bytes 1572868
  206.2 153.5 %reduce-scatter.11.cloned.1.call-start = ((), (), s32[]{:S(2)}) async-start(), calls=%async_computation.10 | async-start | bytes 1179648 | tf_op jit(solution)/shard_map/reduce_scatter | solution.py:138
  209.7 201.3 %all-reduce.6.cloned.1.call-start = ((), (), s32[]{:S(2)}) async-start(), calls=%async_computation.11 | async-start | bytes 819200 | tf_op jit(solution)/shard_map/psum | solution.py:135
  359.8 112.2 %reduce-scatter.7.cloned.1.call-start = ((), (), s32[]{:S(2)}) async-start(), calls=%async_computation.7 | async-start | bytes 4718592 | tf_op jit(solution)/shard_map/reduce_scatter | solution.py:127
  363.0 1.0 copy-start.1
  363.0 1.2 copy-start.11
  411.0 63.1 %copy-start.18 = (f32[3,3,32,128]{3,2,1,0:T(8,128)S(1)}, f32[3,3,32,128]{3,2,1,0:T(8,128)}, u32[]{:S(2)}) copy-start(f32[3,3,32,128]{3,2,1,0:T(8,128)} %get-tuple-element.46) | copy-start | bytes 442372
  411.0 63.7 %copy-start.19 = (f32[128,256]{1,0:T(8,128)S(1)}, f32[128,256]{1,0:T(8,128)}, u32[]{:S(2)}) copy-start(f32[128,256]{1,0:T(8,128)} %get-tuple-element.47) | copy-start | bytes 393220
Sparse Core Ops, SparseCore 0:
  9.8 59.6 all-gather.2
  72.1 77.0 reduce-scatter.4
  151.3 40.0 all-gather.4
  194.5 75.4 all-reduce.3
  273.1 42.0 reduce-scatter.8
  317.7 41.9 reduce-scatter.10
  362.4 48.5 all-reduce.5
  413.6 58.3 reduce-scatter.6
